TPU v7x, 32 devices: a whole 2x2x4 slice. The times are simulated.
32 devices in a mesh: ctx: 2 (over x), head: 4 (over y, core), rep: 4 (over z).
Axes of the slice: x: 2, y: 2, z: 4, core: 2. Of those that a mesh axis runs over, the one named last changes fastest.
Arguments:
- kv_cache: float32 [8, 2, 512, 8, 128], P('head', None, 'ctx', 'rep'), may hold values from -8 to 8
- prefill_q: float32 [8, 256, 64, 128], P('head', 'ctx', 'rep'), may hold values from -512 to 512
- decode_q: float32 [8, 8, 4, 64, 128], P(None, ('ctx', 'rep'), None, 'head'), may hold values from -512 to 512
- decode_kv: float32 [8, 8, 4, 2, 8, 128], P(None, ('ctx', 'rep'), None, None, 'head'), may hold values from -12 to 12
- lengths: int32 [8], replicated, may hold values from 256 to 512, as said below
- row_length: int32 [8, 8], P(None, ('ctx', 'rep')), may hold values from 2 to 512, as said below
Outputs:
- prefill_out: float32 [8, 256, 64, 128], P('head', 'ctx', 'rep')
- decode_out: float32 [8, 8, 4, 64, 128], P(None, ('ctx', 'rep'), None, 'head')
Inputs may be any that keep to these rules, and one draw needn't show every extreme that they name: `lengths`: multiples of 128; some request has length 512. `row_length`: a row reads at most its request's length; every request has a row that reads its whole length.
All inputs are finite; a program needn't handle non-finite values.
Results may differ from a plain program's by a relative error of at most 0.0003.
Values sent between devices are 32-bit elements; how exact they have to be, the bound alone decides.
No kernel may reach another device: no remote copies, remote signals or barrier semaphores. Data moves between devices by JAX's collectives and lax.ppermute only.
A program may use at most 128 MiB of HBM per device.

v0:
```python
import math
import jax
import jax.numpy as jnp
from jax import lax
from jax.sharding import PartitionSpec as P

NEG_FILL = -1e30
HIGH_PRECISION = lax.Precision.HIGHEST


def broadcast(value, axis, source):
    kept = jnp.where(lax.axis_index(axis) == source, value, 0).astype(value.dtype)
    return lax.psum(kept, axis)


def online_fold(running, scores, value_rows, pattern):
    run_max, run_total, run_acc = running
    new_max = jnp.maximum(run_max, jnp.max(scores, axis=-1))
    weights = jnp.exp(scores - new_max[..., None])
    new_total = jnp.sum(weights, axis=-1)
    new_acc = jnp.einsum(pattern, weights, value_rows, precision=HIGH_PRECISION)
    return (new_max, new_total, new_acc)


def empty_state(lead_shape, head_dim):
    return (
        jnp.full(lead_shape, NEG_FILL, jnp.float32),
        jnp.zeros(lead_shape, jnp.float32),
        jnp.zeros(lead_shape + (head_dim,), jnp.float32),
    )


def block_fold(running, query_rows, key_block, first_pos, limits, score_scale, strict):
    block_len = key_block.shape[2]
    scores = (
        jnp.einsum("bkrd,bnkd->bkrn", query_rows, key_block[:, 0], precision=HIGH_PRECISION)
        * score_scale
    )
    positions = first_pos + jnp.arange(block_len, dtype=jnp.int32)
    if strict:
        allowed = positions[None, None, :] < limits[:, :, None]
    else:
        allowed = positions[None, None, :] <= limits[:, :, None]
    scores = jnp.where(allowed[:, None], scores, NEG_FILL)
    return online_fold(running, scores, key_block[:, 1], "bkrn,bnkd->bkrd")


def source_major(values, slot_count, kv_heads, sources, count_rows, step_count, group_size):
    tail_shape = values.shape[3:]
    spread_out = values.reshape(
        (slot_count, kv_heads, sources, count_rows, step_count, group_size) + tail_shape
    )
    axes_order = (2, 0, 3, 4, 1, 5) + tuple(range(6, 6 + len(tail_shape)))
    moved = jnp.transpose(spread_out, axes_order)
    return moved.reshape(
        (sources, slot_count, count_rows, step_count, kv_heads * group_size) + tail_shape
    )


def on_device(kv_cache, prefill_q, decode_q, decode_kv, lengths, row_length):
    ctx_count = lax.axis_size("ctx")
    ctx_index = lax.axis_index("ctx")
    head_index = lax.axis_index("head")
    req_group, span_rows, rep_heads, head_dim = prefill_q.shape
    rep_kv = kv_cache.shape[3]
    group_size = rep_heads // rep_kv
    block_len = kv_cache.shape[2]
    score_scale = 1.0 / math.sqrt(head_dim)
    group_lengths = lax.dynamic_slice_in_dim(lengths, head_index * req_group, req_group)
    span_pos = (
        group_lengths[:, None]
        - span_rows * ctx_count
        + ctx_index * span_rows
        + jnp.arange(span_rows, dtype=jnp.int32)[None, :]
    )
    row_pos = jnp.repeat(span_pos, group_size, axis=1)
    prefill_rows = jnp.transpose(
        prefill_q.reshape(req_group, span_rows, rep_kv, group_size, head_dim), (0, 2, 1, 3, 4)
    ).reshape(req_group, rep_kv, span_rows * group_size, head_dim)
    start_state = empty_state((req_group, rep_kv, span_rows * group_size), head_dim)
    run_max, run_total, run_acc = block_fold(
        start_state,
        prefill_rows,
        lax.all_gather(kv_cache, "ctx", axis=2, tiled=True),
        jnp.int32(0),
        row_pos,
        score_scale,
        False,
    )
    prefill_vals = run_acc / run_total[..., None]
    prefill_out = jnp.transpose(
        prefill_vals.reshape(req_group, rep_kv, span_rows, group_size, head_dim), (0, 2, 1, 3, 4)
    ).reshape(prefill_q.shape)
    all_requests = lax.all_gather(kv_cache, "head", axis=0, tiled=True)
    head_cache = broadcast(all_requests, "rep", head_index)
    requests, row_count, step_count, local_heads, unused_dim = decode_q.shape
    kv_heads = local_heads // group_size
    gathered_rows, gathered_limits = (
        lax.all_gather(decode_q, "ctx", axis=1, tiled=True),
        lax.all_gather(row_length, "ctx", axis=1, tiled=True),
    )
    total_rows = gathered_rows.shape[1]
    grouped = jnp.transpose(
        gathered_rows.reshape(requests, total_rows, step_count, kv_heads, group_size, head_dim),
        (0, 3, 1, 2, 4, 5),
    ).reshape(requests, kv_heads, -1, head_dim)
    limits = jnp.broadcast_to(
        gathered_limits[:, :, None, None], (requests, total_rows, step_count, group_size)
    ).reshape(requests, -1)
    running = empty_state((requests, kv_heads, grouped.shape[2]), head_dim)
    running = block_fold(
        running, grouped, head_cache, ctx_index * block_len, limits, score_scale, True
    )
    shaped = tuple(
        (
            source_major(values, requests, kv_heads, ctx_count, row_count, step_count, group_size)
            for values in running
        )
    )
    home_max, home_total, home_acc = (
        lax.all_to_all(shaped[0], "ctx", split_axis=0, concat_axis=0, tiled=True),
        lax.all_to_all(shaped[1], "ctx", split_axis=0, concat_axis=0, tiled=True),
        lax.all_to_all(shaped[2], "ctx", split_axis=0, concat_axis=0, tiled=True),
    )
    ctx_max = jnp.max(home_max, axis=0)
    factor = jnp.exp(home_max - ctx_max[None])
    ctx_total = jnp.sum(home_total * factor, axis=0)
    ctx_acc = jnp.sum(home_acc * factor[..., None], axis=0)
    home_rows = decode_q.reshape(requests, row_count, step_count, kv_heads, group_size, head_dim)
    draft_scores = (
        jnp.einsum(
            "artkgd,arskd->artkgs", home_rows, decode_kv[:, :, :, 0], precision=HIGH_PRECISION
        )
        * score_scale
    )
    step_ids = jnp.arange(step_count, dtype=jnp.int32)
    causal = step_ids[None, :] <= step_ids[:, None]
    draft_scores = jnp.where(causal[None, None, :, None, None, :], draft_scores, NEG_FILL)
    ctx_max = ctx_max.reshape(requests, row_count, step_count, kv_heads, group_size)
    ctx_total = ctx_total.reshape(requests, row_count, step_count, kv_heads, group_size)
    ctx_acc = ctx_acc.reshape(requests, row_count, step_count, kv_heads, group_size, head_dim)
    joint_max = jnp.maximum(ctx_max, jnp.max(draft_scores, axis=-1))
    draft_weights = jnp.exp(draft_scores - joint_max[..., None])
    ctx_factor = jnp.exp(ctx_max - joint_max)
    denominator = ctx_total * ctx_factor + jnp.sum(draft_weights, axis=-1)
    numerator = ctx_acc * ctx_factor[..., None] + jnp.einsum(
        "artkgs,arskd->artkgd", draft_weights, decode_kv[:, :, :, 1], precision=HIGH_PRECISION
    )
    decode_out = (numerator / denominator[..., None]).reshape(decode_q.shape)
    return (prefill_out, decode_out)


def solution(mesh):
    in_specs = (
        P("head", None, "ctx", "rep", None),
        P("head", "ctx", "rep", None),
        P(None, ("ctx", "rep"), None, "head", None),
        P(None, ("ctx", "rep"), None, None, "head", None),
        P(),
        P(None, ("ctx", "rep")),
    )
    out_specs = (P("head", "ctx", "rep", None), P(None, ("ctx", "rep"), None, "head", None))
    return jax.shard_map(
        on_device, mesh=mesh, in_specs=in_specs, out_specs=out_specs, check_vma=False
    )
```

profile of v0, /device:TPU:0, one launch (start us, length us, event | category | flops | bytes accessed | tf_op | source)
XLA Modules:
  0.0 285.3 jit_solution(5755422686790085839)
XLA Ops:
  7.2 2.4 copy.82
  9.7 0.7 all-gather.4.cloned.1.call-update
  10.5 36.9 %all-gather.6.cloned.1.call-done = f32[8,2,256,2,128]{4,2,3,0,1:T(8,128)} async-done(((f32[2,2,256,2,128]{4,2,3,0,1:T(8,128)}), f32[8,2,256,2,128]{4,2,3,0,1:T(8,128)}) %all-gather.6.cloned.1.call-update) | async-done | bytes 4194320 | tf_op jit(solution)/shard_map/all_gather | solution.py:94
  47.4 4.6 %broadcast_select_fusion = f32[8,2,256,2,128]{4,2,3,0,1:T(8,128)} fusion(f32[8,2,256,2,128]{4,2,3,0,1:T(8,128)} %all-gather.6.cloned.1.call-done, pred[]{:T(512)S(6)} %eq.3), kind=kLoop, calls=%fused_computation.18 | loop fusion | flops 1048576 | bytes 8388609 | tf_op jit(solution)/shard_map/jit(_where)/select_n | solution.py:12
  52.0 0.6 copy-done.5
  52.6 4.2 %all-gather = s32[2,1,8]{2,1,0:T(1,128)S(1)} all-gather(s32[1,1,8]{2,1,0:T(1,128)S(1)} %bitcast.147), channel_id=1, replica_groups=mesh['ctx'=2,'head'=4,'rep'=4] {'ctx'}, dimensions={0}, use_global_device_ids=true | all-gather | bytes 96 | tf_op jit(solution)/shard_map/all_gather | solution.py:100
  57.5 12.6 %all_gather.15 = f32[8,2,4,16,128]{4,3,2,1,0:T(8,128)S(1)} all-gather(f32[8,1,4,16,128]{4,3,2,1,0:T(8,128)S(1)} %copy-done.1), channel_id=1, replica_groups=mesh['ctx'=2,'head'=4,'rep'=4] {'ctx'}, dimensions={1}, use_global_device_ids=true | all-gather | bytes 786432 | tf_op jit(solution)/shard_map/all_gather | solution.py:99
  70.0 0.9 copy.87
  71.1 3.6 %fusion.31 = (f32[8,4,2,8]{3,1,2,0:T(4,128)S(1)}, f32[8,1,4,2,8,4]{4,5,2,3,0,1:T(4,128)S(1)}) fusion(f32[8,1,4,1,2,128]{5,4,3,2,1,0:T(2,128)S(1)} %get-tuple-element.13, pred[4,4]{1,0:T(4,128)(4,1)S(1)} %iota_compare_fusion.1, f32[8,1,4,16,128]{4,3,2,1,0:T(8,128)S(1)} %copy-done.1), kind=kOutput, calls=%fused_computation.63 | convolution fusion | flops 3151360 | bytes 305168 | tf_op jit(solution)/shard_map/artkgd,arskd->artkgs/dot_general | solution.py:131
  74.7 0.6 iota_compare_fusion
  75.3 10.6 %all-gather.4.cloned.1.call-done = f32[2,2,512,2,128]{4,2,3,0,1:T(8,128)} async-done(((f32[2,2,256,2,128]{4,2,3,0,1:T(8,128)}), f32[2,2,512,2,128]{4,2,3,0,1:T(8,128)}) %all-gather.4.cloned.1.call-update) | async-done | bytes 2097168 | tf_op jit(solution)/shard_map/all_gather | solution.py:84
  86.0 9.6 %fusion = (f32[2,2,1024]{2,1,0:T(2,128)S(1)}, f32[2,2,1024,512]{2,3,1,0:T(8,128)S(1)}) fusion(pred[2,1024,512]{1,2,0:T(8,128)(4,1)S(1)} %iota_compare_fusion, f32[2,2,512,2,128]{4,2,3,0,1:T(8,128)} %all-gather.4.cloned.1.call-done, f32[2,128,16,128]{3,2,1,0:T(8,128)S(1)} %copy-done), kind=kOutput, calls=%fused_computation.2 | convolution fusion | flops 3227512832 | bytes 12599296 | tf_op jit(solution)/shard_map/bkrd,bnkd->bkrn/dot_general | solution.py:36
  95.6 2.2 fusion.1
  97.8 15.4 %divide_bitcast_fusion = f32[2,128,2,8,128]{4,3,1,2,0:T(8,128)S(1)} fusion(f32[2,2,1024]{2,1,0:T(2,128)S(1)} %fusion.1, f32[2,2,512,2,128]{4,2,3,0,1:T(8,128)S(1)} %copy-done.2, f32[2,2,1024,512]{2,3,1,0:T(8,128)S(1)} %get-tuple-element.17, f32[2,2,1024]{2,1,0:T(2,128)S(1)} %broadcast_maximum_fusion, pred[2,1024,512]{1,2,0:T(8,128)(4,1)S(1)} %iota_compare_fusion), kind=kOutput, calls=%fused_computation.19 | convolution fusion | flops 3228041216 | bytes 12615680 | tf_op jit(solution)/shard_map/bkrn,bnkd->bkrd/dot_general | solution.py:21
  113.3 1.5 copy.141
  114.8 130.5 %all-reduce.2.cloned.1.call-done = f32[8,2,256,2,128]{4,2,3,0,1:T(8,128)} async-done(((f32[8,2,256,2,128]{4,2,3,0,1:T(8,128)}), f32[8,2,256,2,128]{4,2,3,0,1:T(8,128)}) %all-reduce.2.cloned.1.call-update) | async-done | bytes 4194320 | tf_op jit(solution)/shard_map/psum | solution.py:13
  245.2 4.1 %fusion.30 = (f32[8,2,64]{2,1,0:T(2,128)S(1)}, f32[8,2,64,256]{3,2,1,0:T(8,128)S(1)}) fusion(f32[8,2,64,128]{3,2,1,0:T(8,128)} %bitcast.142, f32[8,2,256,2,128]{4,2,3,0,1:T(8,128)} %all-reduce.2.cloned.1.call-done, pred[8,64,256]{2,1,0:T(8,128)(4,1)S(1)} %broadcast_compare_fusion), kind=kOutput, calls=%fused_computation.62 | convolution fusion | flops 403438592 | bytes 3805184 | tf_op jit(solution)/shard_map/bkrd,bnkd->bkrn/dot_general | solution.py:36
  249.4 0.4 fusion.19
  250.1 0.7 reshape.235
  250.8 3.2 %all-to-all-start.2 = ((f32[2,1,512]{2,1,0:T(1,128)}), f32[2,1,512]{2,1,0:T(1,128)S(1)}, u32[]{:S(2)}, u32[]{:S(2)}) async-start(f32[2,1,512]{2,1,0:T(1,128)} %reshape.235), calls=%async_computation.2 | async-start | bytes 8192 | tf_op jit(solution)/shard_map/all_to_all | solution.py:122
  254.3 0.7 reshape.233
  255.0 2.8 all-to-all-done.2
  257.8 3.2 %all-to-all-start.1 = ((f32[2,1,512]{2,1,0:T(1,128)}), f32[2,1,512]{2,1,0:T(1,128)S(1)}, u32[]{:S(2)}, u32[]{:S(2)}) async-start(f32[2,1,512]{2,1,0:T(1,128)} %reshape.233), calls=%async_computation.1 | async-start | bytes 8192 | tf_op jit(solution)/shard_map/all_to_all | solution.py:121
  261.0 3.3 %fusion.7 = f32[8,2,64,128]{3,2,1,0:T(8,128)S(1)} fusion(f32[8,2,256,2,128]{4,2,3,0,1:T(8,128)} %all-reduce.2.cloned.1.call-done, f32[8,2,64,256]{3,2,1,0:T(8,128)S(1)} %get-tuple-element.19, f32[8,2,64]{2,1,0:T(2,128)S(1)} %broadcast_maximum_fusion.1), kind=kOutput, calls=%fused_computation.11 | convolution fusion | flops 402915328 | bytes 3674112 | tf_op jit(solution)/shard_map/bkrn,bnkd->bkrd/dot_general | solution.py:21
  264.3 0.8 copy.142
  265.2 0.6 broadcast.71
  265.8 0.7 reduce.6
  266.6 3.5 %all-to-all-start = ((f32[2,8,1,4,16,128]{5,4,3,1,2,0:T(8,128)}), f32[2,8,1,4,16,128]{5,4,3,1,2,0:T(8,128)S(1)}, u32[]{:S(2)}, u32[]{:S(2)}) async-start(f32[2,8,1,4,16,128]{5,4,3,1,2,0:T(8,128)} %bitcast.137), calls=%async_computation | async-start | bytes 1048576 | tf_op jit(solution)/shard_map/all_to_all | solution.py:123
  270.1 0.7 reduce.5
  271.3 5.9 %all-to-all-done = f32[2,8,1,4,16,128]{5,4,3,1,2,0:T(8,128)S(1)} async-done(((f32[2,8,1,4,16,128]{5,4,3,1,2,0:T(8,128)}), f32[2,8,1,4,16,128]{5,4,3,1,2,0:T(8,128)S(1)}, u32[]{:S(2)}, u32[]{:S(2)}) %all-to-all-start) | async-done | bytes 524320 | tf_op jit(solution)/shard_map/all_to_all | solution.py:123
  277.3 0.7 fusion.16
  278.0 0.7 copy.143
  (51 shorter events, 2.3 us)
Async XLA Ops:
  7.2 78.8 %copy-start = (f32[2,128,16,128]{3,2,1,0:T(8,128)S(1)}, f32[2,128,16,128]{3,2,1,0:T(8,128)}, u32[]{:S(2)}) copy-start(f32[2,128,16,128]{3,2,1,0:T(8,128)} %param.7) | copy-start | bytes 6291460
  7.2 40.2 %all-gather.6.cloned.1.call-start = ((), (), s32[]{:S(2)}) async-start(), calls=%async_computation.4 | async-start | bytes 5242880 | tf_op jit(solution)/shard_map/all_gather | solution.py:94
  9.7 76.3 %all-gather.4.cloned.1.call-start = ((), (), s32[]{:S(2)}) async-start(), calls=%async_computation.3 | async-start | bytes 3145728 | tf_op jit(solution)/shard_map/all_gather | solution.py:84
  10.4 234.8 %all-reduce.2.cloned.1.call-start = ((), (), s32[]{:S(2)}) async-start(), calls=%async_computation.5 | async-start | bytes 8388608 | tf_op jit(solution)/shard_map/psum | solution.py:13
  52.0 0.7 copy-start.5
  52.0 5.1 %copy-start.4 = (s32[8]{0:T(128)S(1)}, s32[8]{0:T(128)}, u32[]{:S(2)}) copy-start(s32[8]{0:T(128)} %param.10) | copy-start | bytes 100
  52.0 5.5 %copy-start.1 = (f32[8,1,4,16,128]{4,3,2,1,0:T(8,128)S(1)}, f32[8,1,4,16,128]{4,3,2,1,0:T(8,128)}, u32[]{:S(2)}) copy-start(f32[8,1,4,16,128]{4,3,2,1,0:T(8,128)} %param.8) | copy-start | bytes 786436
  52.0 19.0 %copy-start.3 = (f32[8,1,4,2,2,128]{5,4,3,2,1,0:T(2,128)S(1)}, f32[8,1,4,2,2,128]{5,4,3,2,1,0:T(2,128)}, u32[]{:S(2)}) copy-start(f32[8,1,4,2,2,128]{5,4,3,2,1,0:T(2,128)} %param.9) | copy-start | bytes 196612
  95.6 2.2 copy-start.2
  250.8 7.0 %all-to-all-start.2 = ((f32[2,1,512]{2,1,0:T(1,128)}), f32[2,1,512]{2,1,0:T(1,128)S(1)}, u32[]{:S(2)}, u32[]{:S(2)}) async-start(f32[2,1,512]{2,1,0:T(1,128)} %reshape.235), calls=%async_computation.2 | async-start | bytes 8192 | tf_op jit(solution)/shard_map/all_to_all | solution.py:122
  257.8 8.8 %all-to-all-start.1 = ((f32[2,1,512]{2,1,0:T(1,128)}), f32[2,1,512]{2,1,0:T(1,128)S(1)}, u32[]{:S(2)}, u32[]{:S(2)}) async-start(f32[2,1,512]{2,1,0:T(1,128)} %reshape.233), calls=%async_computation.1 | async-start | bytes 8192 | tf_op jit(solution)/shard_map/all_to_all | solution.py:121
  266.6 10.6 %all-to-all-start = ((f32[2,8,1,4,16,128]{5,4,3,1,2,0:T(8,128)}), f32[2,8,1,4,16,128]{5,4,3,1,2,0:T(8,128)S(1)}, u32[]{:S(2)}, u32[]{:S(2)}) async-start(f32[2,8,1,4,16,128]{5,4,3,1,2,0:T(8,128)} %bitcast.137), calls=%async_computation | async-start | bytes 1048576 | tf_op jit(solution)/shard_map/all_to_all | solution.py:123
Sparse Core Ops, SparseCore 0:
  10.2 37.1 all-gather.5
  49.5 36.4 all-gather.3
  88.4 156.8 all-reduce.1
where the time goes:
time: 286 us; the launch traced here: 285 us
  waiting for transfers between devices  187 us (65%)
  matrix products  36.7 us (13%)
  blocking collectives  16.8 us (6%)
  between operations  14 us (5%)
  local copies, waits for them, and re-layouts  10.3 us (4%)
  starting transfers between devices  10 us (3%)
  other arithmetic  10 us (3%)
    psum x1, waiting for transfers between devices, broadcast(): return lax.psum(kept, axis)  130 us
    all_gather x1, waiting for transfers between devices, on_device(): all_requests = lax.all_gather(kv_cache, 'head', axis=0, tiled=True)  36.9 us
    dot_general x2, matrix products, online_fold(): new_acc = jnp.einsum(pattern, weights, value_rows, precision=HIGH_PRECISION)  18.8 us
    dot_general x2, matrix products, block_fold(): jnp.einsum('bkrd,bnkd->bkrn', query_rows, key_block[:, 0], precision=HIGH...  13.7 us
    all_gather x1, blocking collectives, on_device(): lax.all_gather(decode_q, 'ctx', axis=1, tiled=True)  12.6 us
    all_gather x1, waiting for transfers between devices, on_device(): lax.all_gather(kv_cache, 'ctx', axis=2, tiled=True)  10.6 us
    all_to_all x1, waiting for transfers between devices, on_device(): lax.all_to_all(shaped[2], 'ctx', split_axis=0, concat_axis=0, tiled=True)  5.85 us
  transfers between devices with their start and end apart: 6, of which 5 were waited for; matrix products, arithmetic and copies ran while one was open for 16% of the time, Pallas kernels for 0%

commit v1 on v0

--- a/solution.py
+++ b/solution.py
@@ -91,7 +91,12 @@
     prefill_out = jnp.transpose(
         prefill_vals.reshape(req_group, rep_kv, span_rows, group_size, head_dim), (0, 2, 1, 3, 4)
     ).reshape(prefill_q.shape)
-    all_requests = lax.all_gather(kv_cache, "head", axis=0, tiled=True)
+    ring = [kv_cache]
+    for hop in range(3):
+        ring.append(lax.ppermute(ring[-1], "head", [(dev, (dev + 1) % 4) for dev in range(4)]))
+    all_requests = jnp.roll(
+        jnp.concatenate(ring[::-1], axis=0), (lax.axis_index("head") + 1) * ring[0].shape[0], axis=0
+    )
     head_cache = broadcast(all_requests, "rep", head_index)
     requests, row_count, step_count, local_heads, unused_dim = decode_q.shape
     kv_heads = local_heads // group_size

time: 286 us -> 264 us (0.923)
  waiting for transfers between devices: 187 us -> 155 us
  local copies, waits for them, and re-layouts: 10.3 us -> 18 us
    ppermute x0 -> x3, waiting for transfers between devices: none -> 43.4 us  [on_device(): lax.ppermute(ring[-1], 'head', [(dev, (dev + 1) % 4) for dev in range(4)])]
    all_gather x1 -> x0, waiting for transfers between devices: 36.9 us -> none  [on_device(): all_requests = lax.all_gather(kv_cache, 'head', axis=0, tiled=True)]
    psum x1, waiting for transfers between devices: 130 us -> 103 us  [broadcast(): return lax.psum(kept, axis)]
    all_gather x1, waiting for transfers between devices: 10.6 us -> 0.02 us  [on_device(): lax.all_gather(kv_cache, 'ctx', axis=2, tiled=True)]
    unnamed x20 -> x37, local copies, waits for them, and re-layouts: 4.68 us -> 11.7 us
  transfers between devices with their start and end apart: 6 -> 8, of which waited for: 5 -> 6; matrix products, arithmetic and copies ran while one was open for 16% -> 20% of each run, Pallas kernels for 0% -> 0%
where the time goes in v1:
time: 264 us; the launch traced here: 263 us
  waiting for transfers between devices  155 us (59%)
  matrix products  38.2 us (14%)
  local copies, waits for them, and re-layouts  18 us (7%)
  blocking collectives  17.1 us (6%)
  between operations  15.9 us (6%)
  starting transfers between devices  10.5 us (4%)
  other arithmetic  8.33 us (3%)
    psum x1, waiting for transfers between devices, broadcast(): return lax.psum(kept, axis)  103 us
    ppermute x3, waiting for transfers between devices, on_device(): lax.ppermute(ring[-1], 'head', [(dev, (dev + 1) % 4) for dev in range(4)])  43.4 us
    dot_general x2, matrix products, online_fold(): new_acc = jnp.einsum(pattern, weights, value_rows, precision=HIGH_PRECISION)  18.7 us
    dot_general x2, matrix products, block_fold(): jnp.einsum('bkrd,bnkd->bkrn', query_rows, key_block[:, 0], precision=HIGH...  13.9 us
    all_gather x1, blocking collectives, on_device(): lax.all_gather(decode_q, 'ctx', axis=1, tiled=True)  12.7 us
    unnamed x37, local copies, waits for them, and re-layouts  11.7 us
    all_to_all x1, waiting for transfers between devices, on_device(): lax.all_to_all(shaped[2], 'ctx', split_axis=0, concat_axis=0, tiled=True)  5.74 us
  transfers between devices with their start and end apart: 8, of which 6 were waited for; matrix products, arithmetic and copies ran while one was open for 20% of the time, Pallas kernels for 0%

profile of v1, /device:TPU:0, one launch (start us, length us, event | category | flops | bytes accessed | tf_op | source)
XLA Modules:
  0.0 263.1 jit_solution(4128421607211375304)
XLA Ops:
  8.1 2.5 copy.90
  11.0 14.6 %collective-permute-done = f32[2,2,256,2,128]{4,2,3,0,1:T(8,128)S(1)} collective-permute-done((f32[2,2,256,2,128]{4,2,3,0,1:T(8,128)}, f32[2,2,256,2,128]{4,2,3,0,1:T(8,128)S(1)}, u32[]{:S(2)}, u32[]{:S(2)}) %collective-permute-start) | collective-permute-done | bytes 1048608 | tf_op jit(solution)/shard_map/ppermute | solution.py:96
  25.6 1.0 copy-done.2
  26.7 14.3 %collective-permute-done.1 = f32[2,2,256,2,128]{4,2,3,0,1:T(8,128)} collective-permute-done((f32[2,2,256,2,128]{4,2,3,0,1:T(8,128)S(1)}, f32[2,2,256,2,128]{4,2,3,0,1:T(8,128)}, u32[]{:S(2)}, u32[]{:S(2)}) %collective-permute-start.1) | collective-permute-done | bytes 1048608 | tf_op jit(solution)/shard_map/ppermute | solution.py:96
  41.1 14.4 %collective-permute-done.2 = f32[2,2,256,2,128]{4,2,3,0,1:T(8,128)} collective-permute-done((f32[2,2,256,2,128]{4,2,3,0,1:T(8,128)}, f32[2,2,256,2,128]{4,2,3,0,1:T(8,128)}, u32[]{:S(2)}, u32[]{:S(2)}) %collective-permute-start.2) | collective-permute-done | bytes 1048608 | tf_op jit(solution)/shard_map/ppermute | solution.py:96
  55.5 1.3 constant_dynamic-update-slice_fusion.7
  56.8 1.3 constant_dynamic-update-slice_fusion.6
  58.1 1.3 constant_dynamic-update-slice_fusion.5
  59.5 1.3 constant_dynamic-update-slice_fusion.3
  60.8 1.3 constant_dynamic-update-slice_fusion.2
  62.3 2.3 dynamic-slice_select_fusion
  64.6 4.4 %all-gather = s32[2,1,8]{2,1,0:T(1,128)S(1)} all-gather(s32[1,1,8]{2,1,0:T(1,128)S(1)} %bitcast.147), channel_id=1, replica_groups=mesh['ctx'=2,'head'=4,'rep'=4] {'ctx'}, dimensions={0}, use_global_device_ids=true | all-gather | bytes 96 | tf_op jit(solution)/shard_map/all_gather | solution.py:105
  69.3 12.7 %all_gather.11 = f32[8,2,4,16,128]{4,3,2,1,0:T(8,128)S(1)} all-gather(f32[8,1,4,16,128]{4,3,2,1,0:T(8,128)S(1)} %copy-done.4), channel_id=1, replica_groups=mesh['ctx'=2,'head'=4,'rep'=4] {'ctx'}, dimensions={1}, use_global_device_ids=true | all-gather | bytes 786432 | tf_op jit(solution)/shard_map/all_gather | solution.py:104
  82.0 0.9 copy.97
  83.9 0.8 broadcast_compare_fusion
  84.7 4.2 %fusion.31 = (f32[8,4,2,8]{3,1,2,0:T(4,128)}, f32[8,1,4,2,8,4]{4,5,2,3,0,1:T(4,128)S(1)}) fusion(f32[8,1,4,1,2,128]{5,4,3,2,1,0:T(2,128)S(1)} %get-tuple-element.13, pred[4,4]{1,0:T(4,128)(4,1)S(1)} %iota_compare_fusion.1, f32[8,1,4,16,128]{4,3,2,1,0:T(8,128)S(1)} %copy-done.4), kind=kOutput, calls=%fused_computation.71 | convolution fusion | flops 3151360 | bytes 305168 | tf_op jit(solution)/shard_map/artkgd,arskd->artkgs/dot_general | solution.py:136
  89.6 9.7 %fusion = (f32[2,2,1024]{2,1,0:T(2,128)S(1)}, f32[2,2,1024,512]{2,3,1,0:T(8,128)S(1)}) fusion(pred[2,1024,512]{1,2,0:T(8,128)(4,1)S(1)} %iota_compare_fusion, f32[2,2,512,2,128]{4,2,3,0,1:T(8,128)} %all-gather.3.cloned.1.call-done, f32[2,128,16,128]{3,2,1,0:T(8,128)S(1)} %copy-done), kind=kOutput, calls=%fused_computation.2 | convolution fusion | flops 3227512832 | bytes 12599296 | tf_op jit(solution)/shard_map/bkrd,bnkd->bkrn/dot_general | solution.py:36
  99.3 2.2 fusion.1
  101.6 15.4 %divide_bitcast_fusion = f32[2,128,2,8,128]{4,3,1,2,0:T(8,128)S(1)} fusion(f32[2,2,1024]{2,1,0:T(2,128)S(1)} %fusion.1, f32[2,2,512,2,128]{4,2,3,0,1:T(8,128)S(1)} %copy-done.5, f32[2,2,1024,512]{2,3,1,0:T(8,128)S(1)} %get-tuple-element.17, f32[2,2,1024]{2,1,0:T(2,128)S(1)} %broadcast_maximum_fusion, pred[2,1024,512]{1,2,0:T(8,128)(4,1)S(1)} %iota_compare_fusion), kind=kOutput, calls=%fused_computation.19 | convolution fusion | flops 3228041216 | bytes 12615680 | tf_op jit(solution)/shard_map/bkrn,bnkd->bkrd/dot_general | solution.py:21
  117.0 1.5 copy.153
  118.5 103.0 %all-reduce.2.cloned.1.call-done = f32[8,2,256,2,128]{4,2,3,0,1:T(8,128)} async-done(((f32[8,2,256,2,128]{4,2,3,0,1:T(8,128)}), f32[8,2,256,2,128]{4,2,3,0,1:T(8,128)}) %all-reduce.2.cloned.1.call-update) | async-done | bytes 4194320 | tf_op jit(solution)/shard_map/psum | solution.py:13
  221.5 4.1 %fusion.30 = (f32[8,2,64]{2,1,0:T(2,128)S(1)}, f32[8,2,64,256]{3,2,1,0:T(8,128)S(1)}) fusion(f32[8,2,64,128]{3,2,1,0:T(8,128)} %bitcast.142, f32[8,2,256,2,128]{4,2,3,0,1:T(8,128)} %all-reduce.2.cloned.1.call-done, pred[8,64,256]{2,1,0:T(8,128)(4,1)S(1)} %copy-done.6), kind=kOutput, calls=%fused_computation.70 | convolution fusion | flops 403438592 | bytes 3805184 | tf_op jit(solution)/shard_map/bkrd,bnkd->bkrn/dot_general | solution.py:36
  227.1 3.2 %all-to-all-start.2 = ((f32[2,1,512]{2,1,0:T(1,128)}), f32[2,1,512]{2,1,0:T(1,128)S(1)}, u32[]{:S(2)}, u32[]{:S(2)}) async-start(f32[2,1,512]{2,1,0:T(1,128)} %reshape.235), calls=%async_computation.2 | async-start | bytes 8192 | tf_op jit(solution)/shard_map/all_to_all | solution.py:127
  231.2 2.8 %all-to-all-done.2 = f32[2,1,512]{2,1,0:T(1,128)S(1)} async-done(((f32[2,1,512]{2,1,0:T(1,128)}), f32[2,1,512]{2,1,0:T(1,128)S(1)}, u32[]{:S(2)}, u32[]{:S(2)}) %all-to-all-start.2) | async-done | bytes 4128 | tf_op jit(solution)/shard_map/all_to_all | solution.py:127
  234.1 3.2 %all-to-all-start.1 = ((f32[2,1,512]{2,1,0:T(1,128)}), f32[2,1,512]{2,1,0:T(1,128)S(1)}, u32[]{:S(2)}, u32[]{:S(2)}) async-start(f32[2,1,512]{2,1,0:T(1,128)} %reshape.233), calls=%async_computation.1 | async-start | bytes 8192 | tf_op jit(solution)/shard_map/all_to_all | solution.py:126
  237.3 3.3 %fusion.7 = f32[8,2,64,128]{3,2,1,0:T(8,128)S(1)} fusion(f32[8,2,256,2,128]{4,2,3,0,1:T(8,128)} %all-reduce.2.cloned.1.call-done, f32[8,2,64,256]{3,2,1,0:T(8,128)S(1)} %get-tuple-element.19, f32[8,2,64]{2,1,0:T(2,128)S(1)} %broadcast_maximum_fusion.1), kind=kOutput, calls=%fused_computation.12 | convolution fusion | flops 402915328 | bytes 3674112 | tf_op jit(solution)/shard_map/bkrn,bnkd->bkrd/dot_general | solution.py:21
  240.6 0.8 copy.154
  242.8 3.5 %all-to-all-start = ((f32[2,8,1,4,16,128]{5,4,3,1,2,0:T(8,128)}), f32[2,8,1,4,16,128]{5,4,3,1,2,0:T(8,128)S(1)}, u32[]{:S(2)}, u32[]{:S(2)}) async-start(f32[2,8,1,4,16,128]{5,4,3,1,2,0:T(8,128)} %bitcast.137), calls=%async_computation | async-start | bytes 1048576 | tf_op jit(solution)/shard_map/all_to_all | solution.py:128
  246.3 0.7 reduce.5
  247.6 5.7 %all-to-all-done = f32[2,8,1,4,16,128]{5,4,3,1,2,0:T(8,128)S(1)} async-done(((f32[2,8,1,4,16,128]{5,4,3,1,2,0:T(8,128)}), f32[2,8,1,4,16,128]{5,4,3,1,2,0:T(8,128)S(1)}, u32[]{:S(2)}, u32[]{:S(2)}) %all-to-all-start) | async-done | bytes 524320 | tf_op jit(solution)/shard_map/all_to_all | solution.py:128
  253.5 1.4 fusion.16
  254.9 0.7 copy.155
  (72 shorter events, 7.2 us)
Async XLA Ops:
  8.0 81.6 %copy-start = (f32[2,128,16,128]{3,2,1,0:T(8,128)S(1)}, f32[2,128,16,128]{3,2,1,0:T(8,128)}, u32[]{:S(2)}) copy-start(f32[2,128,16,128]{3,2,1,0:T(8,128)} %param.7) | copy-start | bytes 6291460
  8.0 51.4 %copy-start.1 = (f32[2,2,256,2,128]{4,3,2,1,0:T(2,128)S(1)}, f32[2,2,256,2,128]{4,3,2,1,0:T(2,128)}, u32[]{:S(2)}) copy-start(f32[2,2,256,2,128]{4,3,2,1,0:T(2,128)} %param.6) | copy-start | bytes 3145732
  8.0 81.5 %all-gather.3.cloned.1.call-start = ((), (), s32[]{:S(2)}) async-start(), calls=%async_computation.3 | async-start | bytes 3145728 | tf_op jit(solution)/shard_map/all_gather | solution.py:84
  10.5 15.1 %collective-permute-start = (f32[2,2,256,2,128]{4,2,3,0,1:T(8,128)}, f32[2,2,256,2,128]{4,2,3,0,1:T(8,128)S(1)}, u32[]{:S(2)}, u32[]{:S(2)}) collective-permute-start(f32[2,2,256,2,128]{4,2,3,0,1:T(8,128)} %copy.90), channel_id=1, source_target_pairs={{0,4},{4,8},{8,12},{12,0},{1,5},{5,9},{9,13},{13,1},{2,6},{6,10},{... | collective-permute-start | bytes 3145736 | tf_op jit(solution)/shard_map/ppermute | solution.py:96
  25.6 1.0 copy-start.2
  26.6 14.3 %collective-permute-start.1 = (f32[2,2,256,2,128]{4,2,3,0,1:T(8,128)S(1)}, f32[2,2,256,2,128]{4,2,3,0,1:T(8,128)}, u32[]{:S(2)}, u32[]{:S(2)}) collective-permute-start(f32[2,2,256,2,128]{4,2,3,0,1:T(8,128)S(1)} %collective-permute-done), channel_id=1, source_target_pairs={{0,4},{4,8},{8,12},{12,0},{1,5},{5,9},{9,13},{13,1},{2,6},{6,10},{... | collective-permute-start | bytes 3145736 | tf_op jit(solution)/shard_map/ppermute | solution.py:96
  40.9 14.5 %collective-permute-start.2 = (f32[2,2,256,2,128]{4,2,3,0,1:T(8,128)}, f32[2,2,256,2,128]{4,2,3,0,1:T(8,128)}, u32[]{:S(2)}, u32[]{:S(2)}) collective-permute-start(f32[2,2,256,2,128]{4,2,3,0,1:T(8,128)} %collective-permute-done.1), channel_id=1, source_target_pairs={{0,4},{4,8},{8,12},{12,0},{1,5},{5,9},{9,13},{13,1},{2,6},{6,10},{... | collective-permute-start | bytes 3145736 | tf_op jit(solution)/shard_map/ppermute | solution.py:96
  41.0 180.5 %all-reduce.2.cloned.1.call-start = ((), (), s32[]{:S(2)}) async-start(), calls=%async_computation.4 | async-start | bytes 8388608 | tf_op jit(solution)/shard_map/psum | solution.py:13
  41.0 21.0 %copy-start.3 = (f32[2,2,256,2,128]{4,2,3,0,1:T(8,128)S(1)}, f32[2,2,256,2,128]{4,2,3,0,1:T(8,128)}, u32[]{:S(2)}) copy-start(f32[2,2,256,2,128]{4,2,3,0,1:T(8,128)} %copy-done.2) | copy-start | bytes 3145732
  62.1 2.5 copy-start.10
  62.1 7.2 %copy-start.4 = (f32[8,1,4,16,128]{4,3,2,1,0:T(8,128)S(1)}, f32[8,1,4,16,128]{4,3,2,1,0:T(8,128)}, u32[]{:S(2)}) copy-start(f32[8,1,4,16,128]{4,3,2,1,0:T(8,128)} %param.8) | copy-start | bytes 786436
  62.2 20.7 %copy-start.9 = (s32[8]{0:T(128)S(1)}, s32[8]{0:T(128)}, u32[]{:S(2)}) copy-start(s32[8]{0:T(128)} %param.10) | copy-start | bytes 100
  62.2 21.1 %copy-start.8 = (f32[8,1,4,2,2,128]{5,4,3,2,1,0:T(2,128)S(1)}, f32[8,1,4,2,2,128]{5,4,3,2,1,0:T(2,128)}, u32[]{:S(2)}) copy-start(f32[8,1,4,2,2,128]{5,4,3,2,1,0:T(2,128)} %param.9) | copy-start | bytes 196612
  89.6 12.0 %copy-start.5 = (f32[2,2,512,2,128]{4,2,3,0,1:T(8,128)S(1)}, f32[2,2,512,2,128]{4,2,3,0,1:T(8,128)}, u32[]{:S(2)}) copy-start(f32[2,2,512,2,128]{4,2,3,0,1:T(8,128)} %all-gather.3.cloned.1.call-done) | copy-start | bytes 6291460
  101.6 119.9 %copy-start.6 = (pred[8,64,256]{2,1,0:T(8,128)(4,1)S(1)}, pred[8,64,256]{2,1,0:T(8,128)(4,1)}, u32[]{:S(2)}) copy-start(pred[8,64,256]{2,1,0:T(8,128)(4,1)} %broadcast_compare_fusion) | copy-start | bytes 393220
  117.0 130.2 %copy-start.7 = (f32[8,4,2,8]{3,1,2,0:T(4,128)S(1)}, f32[8,4,2,8]{3,1,2,0:T(4,128)}, u32[]{:S(2)}) copy-start(f32[8,4,2,8]{3,1,2,0:T(4,128)} %get-tuple-element.20) | copy-start | bytes 6148
  227.1 7.0 %all-to-all-start.2 = ((f32[2,1,512]{2,1,0:T(1,128)}), f32[2,1,512]{2,1,0:T(1,128)S(1)}, u32[]{:S(2)}, u32[]{:S(2)}) async-start(f32[2,1,512]{2,1,0:T(1,128)} %reshape.235), calls=%async_computation.2 | async-start | bytes 8192 | tf_op jit(solution)/shard_map/all_to_all | solution.py:127
  234.1 8.8 %all-to-all-start.1 = ((f32[2,1,512]{2,1,0:T(1,128)}), f32[2,1,512]{2,1,0:T(1,128)S(1)}, u32[]{:S(2)}, u32[]{:S(2)}) async-start(f32[2,1,512]{2,1,0:T(1,128)} %reshape.233), calls=%async_computation.1 | async-start | bytes 8192 | tf_op jit(solution)/shard_map/all_to_all | solution.py:126
  242.8 10.5 %all-to-all-start = ((f32[2,8,1,4,16,128]{5,4,3,1,2,0:T(8,128)}), f32[2,8,1,4,16,128]{5,4,3,1,2,0:T(8,128)S(1)}, u32[]{:S(2)}, u32[]{:S(2)}) async-start(f32[2,8,1,4,16,128]{5,4,3,1,2,0:T(8,128)} %bitcast.137), calls=%async_computation | async-start | bytes 1048576 | tf_op jit(solution)/shard_map/all_to_all | solution.py:128
Sparse Core Ops, SparseCore 0:
  41.1 39.8 all-gather.2
Sparse Core Ops, SparseCore 1:
  64.7 156.8 all-reduce.1
